TPU v7x, 32 devices: a whole 2x2x4 slice. The times are simulated.
32 devices in a mesh: seq: 4 (over y, x), head: 4 (over z), rows: 2 (over core).
Axes of the slice: x: 2, y: 2, z: 4, core: 2. Of those that a mesh axis runs over, the one named last changes fastest.
Arguments:
- queries: bfloat16 [8, 4, 640, 2048], P('seq', None, 'rows', 'head'), may hold values from -6 to 6
- keys: bfloat16 [8, 4, 640, 2048], P('seq', None, 'rows', 'head'), may hold values from -6 to 6
- values: bfloat16 [8, 4, 640, 2048], P('seq', None, 'rows', 'head'), may hold values from -6 to 6
- counts: int32 [8], replicated, may hold values from 1 to 4, as said below
- rate: float32 [4], P('head'), may hold values from 0.125 to 1
- w_first: bfloat16 [4, 512, 256], P('head'), may hold values from -0.25 to 0.25
- w_third: bfloat16 [4, 512, 256], P('head'), may hold values from -0.25 to 0.25
- w_second: bfloat16 [4, 256, 512], P('head'), may hold values from -0.375 to 0.375
Outputs:
- mixed: bfloat16 [8, 4, 640, 2048], P('seq', None, 'rows', 'head')
Inputs may be any that keep to these rules, and one draw needn't show every extreme that they name: `counts`: taken in order, the sequences fall into consecutive runs, as many as there are groups of 2 sequences, each run with exactly 4 blocks in all; some sequence has 4 blocks.
All inputs are finite; a program needn't handle non-finite values.
Results may differ from a plain program's by a relative error of at most 0.02.
Values may be sent and summed in bfloat16 or wider, within the bound.
A program may use at most 64 MiB of HBM per device.

v0:
```python
import jax
import jax.numpy as jnp
from jax import lax
from jax.sharding import PartitionSpec as P


def normalize_rows(matrix, epsilon):
    matrix = matrix.astype(jnp.float32)
    return matrix * lax.rsqrt(jnp.mean(matrix * matrix, axis=-1, keepdims=True) + epsilon)


def column_norms(weight):
    return jnp.sqrt(jnp.sum(weight * weight, axis=0) + 1e-06)


def rescale(moved, target):
    return moved * (target[None, :] / column_norms(moved)[None, :])


def product(first_op, second_op):
    return jnp.dot(first_op, second_op, preferred_element_type=jnp.float32)


def contract_rows(first_op, second_op):
    return lax.dot_general(
        first_op, second_op, (((0,), (0,)), ((), ())), preferred_element_type=jnp.float32
    )


def against_rows(first_op, second_op):
    return lax.dot_general(
        first_op, second_op, (((1,), (1,)), ((), ())), preferred_element_type=jnp.float32
    )


def partial_sums(current, key_rows, value_rows):
    key_norm = normalize_rows(key_rows, 1e-06).astype(jnp.bfloat16)
    gate_pre = product(key_norm, current[0])
    up_pre = product(key_norm, current[1])
    gate_sig = jax.nn.sigmoid(gate_pre)
    gate_act = gate_pre * gate_sig
    hidden = (gate_act * up_pre).astype(jnp.bfloat16)
    d_hidden = against_rows(value_rows, current[2])
    d_gate = (d_hidden * up_pre * gate_sig * (1.0 + gate_pre * (1.0 - gate_sig))).astype(
        jnp.bfloat16
    )
    d_up = (d_hidden * gate_act).astype(jnp.bfloat16)
    return (
        contract_rows(key_norm, d_gate),
        contract_rows(key_norm, d_up),
        contract_rows(hidden, value_rows),
    )


def answer(current, query_rows):
    query_norm = normalize_rows(query_rows, 1e-06).astype(jnp.bfloat16)
    out_gate = product(query_norm, current[0])
    out_up = product(query_norm, current[1])
    out_hidden = (out_gate * jax.nn.sigmoid(out_gate) * out_up).astype(jnp.bfloat16)
    return normalize_rows(product(out_hidden, current[2]), 1e-05).astype(jnp.bfloat16)


def body(queries, keys, values, counts, rate, w_first, w_third, w_second):
    seq_slots, blocks, block_rows, head_width = queries.shape
    group_index = lax.axis_index("seq")
    row_devices = lax.axis_size("rows")
    step_rate = rate[0] / (block_rows * row_devices)
    initial = (w_first[0], w_third[0], w_second[0])
    full_master = tuple((weight.astype(jnp.float32) for weight in initial))
    full_targets = tuple((column_norms(weight) for weight in full_master))

    def combine(partials):
        return (
            lax.psum(partials[0].astype(jnp.bfloat16), "rows").astype(jnp.float32),
            lax.psum(partials[1].astype(jnp.bfloat16), "rows").astype(jnp.float32),
            lax.psum(partials[2].astype(jnp.bfloat16), "rows").astype(jnp.float32),
        )

    def refresh(master):
        as_bf16 = tuple((weight.astype(jnp.bfloat16) for weight in master))
        return as_bf16

    def advance(state_pair, step_inputs):
        master, current = state_pair
        query_rows, key_rows, value_rows, restart, is_live = step_inputs
        master = tuple(
            (
                jnp.where(restart, fresh_value, kept_value)
                for fresh_value, kept_value in zip(full_master, master)
            )
        )
        current = tuple(
            (
                jnp.where(restart, fresh_value, kept_value)
                for fresh_value, kept_value in zip(initial, current)
            )
        )
        totals = combine(partial_sums(current, key_rows, value_rows))
        moved = tuple(
            (
                rescale(weight + step_rate * grad_total, target)
                for weight, grad_total, target in zip(master, totals, full_targets)
            )
        )
        master = tuple((jnp.where(is_live, new_w, old_w) for new_w, old_w in zip(moved, master)))
        current = refresh(master)
        output = answer(current, query_rows)
        return ((master, current), jnp.where(is_live, output, jnp.zeros_like(output)))

    start_pair = (full_master, initial)
    flat_shape = (seq_slots * blocks, block_rows, head_width)
    block_ids = jnp.arange(blocks, dtype=jnp.int32)
    local_counts = lax.dynamic_slice_in_dim(counts, group_index * seq_slots, seq_slots)
    restart = jnp.tile(block_ids == 0, seq_slots)
    is_live = (block_ids[None, :] < local_counts[:, None]).reshape(-1)
    inputs = (
        queries.reshape(flat_shape),
        keys.reshape(flat_shape),
        values.reshape(flat_shape),
        restart,
        is_live,
    )
    _, outputs = lax.scan(advance, start_pair, inputs)
    return outputs.reshape(queries.shape)


def solution(mesh):
    return jax.shard_map(
        body,
        mesh=mesh,
        in_specs=(
            P("seq", None, "rows", "head"),
            P("seq", None, "rows", "head"),
            P("seq", None, "rows", "head"),
            P(),
            P("head"),
            P("head", None, None),
            P("head", None, None),
            P("head", None, None),
        ),
        out_specs=P("seq", None, "rows", "head"),
        check_vma=False,
    )
```

profile of v0, /device:TPU:13, one launch (start us, length us, event | category | flops | bytes accessed | tf_op | source)
XLA Modules:
  0.0 441.4 jit_solution(3534035693416795645)
XLA Ops:
  16.9 417.6 %while.22 = (s32[]{:T(128)}, f32[512,256]{1,0:T(8,128)S(1)}, f32[512,256]{1,0:T(8,128)S(1)}, f32[256,512]{1,0:T(8,128)S(1)}, bf16[512,256]{1,0:T(8,128)(2,1)S(1)...) while((s32[]{:T(128)}, f32[512,256]{1,0:T(8,128)S(1)}, ...), condition=%wide.region_13.14_spmd, body=%wide.region_3.13_spmd.sunk | while | flops 768313280 | bytes 32221672 | solution.py:123
  32.9 19.6 %all-reduce.5.cloned.1.call-done = (bf16[512,256]{1,0:T(8,128)(2,1)}, bf16[512,256]{1,0:T(8,128)(2,1)}, bf16[256,512]{1,0:T(8,128)(2,1)}) async-done(((bf16[512,256]{1,0:T(8,128)(2,1)}, bf16[512,256]{1,0:T(8,128)(2,1)}, bf16[256,512]{1,0:T(8,128)(2,1)}), (bf16[512,256]{1,0:T(8,128)(2,1)}, bf16[512,256]{1,0:T(8,128)(2,1)}, bf16[256,512]{1,0:T(8,128)(2,1)})) %all-reduce.5.cloned.1.call-update) | async-done | bytes 786448 | tf_op jit(solution)/shard_map/while/body/eval_jaxpr/psum | solution.py:74
  56.2 2.4 fusion.101
  64.7 2.6 multiply_reduce_fusion.12
  67.3 2.6 fusion.104
  85.6 18.9 %all-reduce.5.cloned.1.call-done = (bf16[512,256]{1,0:T(8,128)(2,1)}, bf16[512,256]{1,0:T(8,128)(2,1)}, bf16[256,512]{1,0:T(8,128)(2,1)}) async-done(((bf16[512,256]{1,0:T(8,128)(2,1)}, bf16[512,256]{1,0:T(8,128)(2,1)}, bf16[256,512]{1,0:T(8,128)(2,1)}), (bf16[512,256]{1,0:T(8,128)(2,1)}, bf16[512,256]{1,0:T(8,128)(2,1)}, bf16[256,512]{1,0:T(8,128)(2,1)})) %all-reduce.5.cloned.1.call-update) | async-done | bytes 786448 | tf_op jit(solution)/shard_map/while/body/eval_jaxpr/psum | solution.py:74
  108.3 2.4 fusion.101
  116.8 2.6 multiply_reduce_fusion.12
  119.4 2.6 fusion.104
  137.7 18.9 %all-reduce.5.cloned.1.call-done = (bf16[512,256]{1,0:T(8,128)(2,1)}, bf16[512,256]{1,0:T(8,128)(2,1)}, bf16[256,512]{1,0:T(8,128)(2,1)}) async-done(((bf16[512,256]{1,0:T(8,128)(2,1)}, bf16[512,256]{1,0:T(8,128)(2,1)}, bf16[256,512]{1,0:T(8,128)(2,1)}), (bf16[512,256]{1,0:T(8,128)(2,1)}, bf16[512,256]{1,0:T(8,128)(2,1)}, bf16[256,512]{1,0:T(8,128)(2,1)})) %all-reduce.5.cloned.1.call-update) | async-done | bytes 786448 | tf_op jit(solution)/shard_map/while/body/eval_jaxpr/psum | solution.py:74
  160.4 2.4 fusion.101
  168.8 2.6 multiply_reduce_fusion.12
  171.5 2.6 fusion.104
  189.8 18.9 %all-reduce.5.cloned.1.call-done = (bf16[512,256]{1,0:T(8,128)(2,1)}, bf16[512,256]{1,0:T(8,128)(2,1)}, bf16[256,512]{1,0:T(8,128)(2,1)}) async-done(((bf16[512,256]{1,0:T(8,128)(2,1)}, bf16[512,256]{1,0:T(8,128)(2,1)}, bf16[256,512]{1,0:T(8,128)(2,1)}), (bf16[512,256]{1,0:T(8,128)(2,1)}, bf16[512,256]{1,0:T(8,128)(2,1)}, bf16[256,512]{1,0:T(8,128)(2,1)})) %all-reduce.5.cloned.1.call-update) | async-done | bytes 786448 | tf_op jit(solution)/shard_map/while/body/eval_jaxpr/psum | solution.py:74
  212.4 2.4 fusion.101
  220.9 2.6 multiply_reduce_fusion.12
  223.6 2.6 fusion.104
  242.0 18.9 %all-reduce.5.cloned.1.call-done = (bf16[512,256]{1,0:T(8,128)(2,1)}, bf16[512,256]{1,0:T(8,128)(2,1)}, bf16[256,512]{1,0:T(8,128)(2,1)}) async-done(((bf16[512,256]{1,0:T(8,128)(2,1)}, bf16[512,256]{1,0:T(8,128)(2,1)}, bf16[256,512]{1,0:T(8,128)(2,1)}), (bf16[512,256]{1,0:T(8,128)(2,1)}, bf16[512,256]{1,0:T(8,128)(2,1)}, bf16[256,512]{1,0:T(8,128)(2,1)})) %all-reduce.5.cloned.1.call-update) | async-done | bytes 786448 | tf_op jit(solution)/shard_map/while/body/eval_jaxpr/psum | solution.py:74
  264.6 2.4 fusion.101
  273.1 2.6 multiply_reduce_fusion.12
  275.7 2.6 fusion.104
  294.1 18.9 %all-reduce.5.cloned.1.call-done = (bf16[512,256]{1,0:T(8,128)(2,1)}, bf16[512,256]{1,0:T(8,128)(2,1)}, bf16[256,512]{1,0:T(8,128)(2,1)}) async-done(((bf16[512,256]{1,0:T(8,128)(2,1)}, bf16[512,256]{1,0:T(8,128)(2,1)}, bf16[256,512]{1,0:T(8,128)(2,1)}), (bf16[512,256]{1,0:T(8,128)(2,1)}, bf16[512,256]{1,0:T(8,128)(2,1)}, bf16[256,512]{1,0:T(8,128)(2,1)})) %all-reduce.5.cloned.1.call-update) | async-done | bytes 786448 | tf_op jit(solution)/shard_map/while/body/eval_jaxpr/psum | solution.py:74
  316.7 2.4 fusion.101
  325.2 2.6 multiply_reduce_fusion.12
  327.8 2.6 fusion.104
  346.2 18.9 %all-reduce.5.cloned.1.call-done = (bf16[512,256]{1,0:T(8,128)(2,1)}, bf16[512,256]{1,0:T(8,128)(2,1)}, bf16[256,512]{1,0:T(8,128)(2,1)}) async-done(((bf16[512,256]{1,0:T(8,128)(2,1)}, bf16[512,256]{1,0:T(8,128)(2,1)}, bf16[256,512]{1,0:T(8,128)(2,1)}), (bf16[512,256]{1,0:T(8,128)(2,1)}, bf16[512,256]{1,0:T(8,128)(2,1)}, bf16[256,512]{1,0:T(8,128)(2,1)})) %all-reduce.5.cloned.1.call-update) | async-done | bytes 786448 | tf_op jit(solution)/shard_map/while/body/eval_jaxpr/psum | solution.py:74
  377.3 2.6 multiply_reduce_fusion.12
  379.9 2.6 fusion.104
  398.3 18.9 %all-reduce.5.cloned.1.call-done = (bf16[512,256]{1,0:T(8,128)(2,1)}, bf16[512,256]{1,0:T(8,128)(2,1)}, bf16[256,512]{1,0:T(8,128)(2,1)}) async-done(((bf16[512,256]{1,0:T(8,128)(2,1)}, bf16[512,256]{1,0:T(8,128)(2,1)}, bf16[256,512]{1,0:T(8,128)(2,1)}), (bf16[512,256]{1,0:T(8,128)(2,1)}, bf16[512,256]{1,0:T(8,128)(2,1)}, bf16[256,512]{1,0:T(8,128)(2,1)})) %all-reduce.5.cloned.1.call-update) | async-done | bytes 786448 | tf_op jit(solution)/shard_map/while/body/eval_jaxpr/psum | solution.py:74
  420.9 2.4 fusion.101
  429.4 2.6 multiply_reduce_fusion.12
  432.0 2.6 fusion.104
  (289 shorter events, 216.3 us)
Async XLA Ops:
  6.5 10.2 %copy-start.3 = (bf16[1,512,256]{2,1,0:T(8,128)(2,1)S(1)}, bf16[1,512,256]{2,1,0:T(8,128)(2,1)}, u32[]{:S(2)}) copy-start(bf16[1,512,256]{2,1,0:T(8,128)(2,1)} %param.16) | copy-start | bytes 786436
  6.5 10.2 %copy-start.4 = (bf16[1,512,256]{2,1,0:T(8,128)(2,1)S(1)}, bf16[1,512,256]{2,1,0:T(8,128)(2,1)}, u32[]{:S(2)}) copy-start(bf16[1,512,256]{2,1,0:T(8,128)(2,1)} %param.15) | copy-start | bytes 786436
  17.0 35.5 %all-reduce.5.cloned.1.call-start = ((), (), s32[]{:S(2)}) async-start(), calls=%async_computation | async-start | bytes 1572864 | tf_op jit(solution)/shard_map/while/body/eval_jaxpr/psum | solution.py:74
  17.0 7.9 %copy-start.5 = (bf16[256,512]{1,0:T(8,128)(2,1)S(1)}, bf16[256,512]{1,0:T(8,128)(2,1)}, u32[]{:S(2)}) copy-start(bf16[256,512]{1,0:T(8,128)(2,1)} %get-tuple-element.413) | copy-start | bytes 786436 | tf_op jit(solution)/shard_map/while
  17.0 7.9 %copy-start.6 = (bf16[256,512]{1,0:T(8,128)(2,1)S(1)}, bf16[256,512]{1,0:T(8,128)(2,1)}, u32[]{:S(2)}) copy-start(bf16[256,512]{1,0:T(8,128)(2,1)} %get-tuple-element.381) | copy-start | bytes 786436 | tf_op jit(solution)/shard_map/while
  56.1 4.8 %copy-start.1 = (bf16[512,256]{1,0:T(8,128)(2,1)S(1)}, bf16[512,256]{1,0:T(8,128)(2,1)}, u32[]{:S(2)}) copy-start(bf16[512,256]{1,0:T(8,128)(2,1)} %get-tuple-element.339) | copy-start | bytes 786436 | tf_op jit(solution)/shard_map/while
  69.9 34.7 %all-reduce.5.cloned.1.call-start = ((), (), s32[]{:S(2)}) async-start(), calls=%async_computation | async-start | bytes 1572864 | tf_op jit(solution)/shard_map/while/body/eval_jaxpr/psum | solution.py:74
  69.9 7.8 %copy-start.5 = (bf16[256,512]{1,0:T(8,128)(2,1)S(1)}, bf16[256,512]{1,0:T(8,128)(2,1)}, u32[]{:S(2)}) copy-start(bf16[256,512]{1,0:T(8,128)(2,1)} %get-tuple-element.413) | copy-start | bytes 786436 | tf_op jit(solution)/shard_map/while
  69.9 7.8 %copy-start.6 = (bf16[256,512]{1,0:T(8,128)(2,1)S(1)}, bf16[256,512]{1,0:T(8,128)(2,1)}, u32[]{:S(2)}) copy-start(bf16[256,512]{1,0:T(8,128)(2,1)} %get-tuple-element.381) | copy-start | bytes 786436 | tf_op jit(solution)/shard_map/while
  108.2 4.8 %copy-start.1 = (bf16[512,256]{1,0:T(8,128)(2,1)S(1)}, bf16[512,256]{1,0:T(8,128)(2,1)}, u32[]{:S(2)}) copy-start(bf16[512,256]{1,0:T(8,128)(2,1)} %get-tuple-element.339) | copy-start | bytes 786436 | tf_op jit(solution)/shard_map/while
  122.0 34.6 %all-reduce.5.cloned.1.call-start = ((), (), s32[]{:S(2)}) async-start(), calls=%async_computation | async-start | bytes 1572864 | tf_op jit(solution)/shard_map/while/body/eval_jaxpr/psum | solution.py:74
  122.0 7.8 %copy-start.5 = (bf16[256,512]{1,0:T(8,128)(2,1)S(1)}, bf16[256,512]{1,0:T(8,128)(2,1)}, u32[]{:S(2)}) copy-start(bf16[256,512]{1,0:T(8,128)(2,1)} %get-tuple-element.413) | copy-start | bytes 786436 | tf_op jit(solution)/shard_map/while
  122.0 7.8 %copy-start.6 = (bf16[256,512]{1,0:T(8,128)(2,1)S(1)}, bf16[256,512]{1,0:T(8,128)(2,1)}, u32[]{:S(2)}) copy-start(bf16[256,512]{1,0:T(8,128)(2,1)} %get-tuple-element.381) | copy-start | bytes 786436 | tf_op jit(solution)/shard_map/while
  160.3 4.8 %copy-start.1 = (bf16[512,256]{1,0:T(8,128)(2,1)S(1)}, bf16[512,256]{1,0:T(8,128)(2,1)}, u32[]{:S(2)}) copy-start(bf16[512,256]{1,0:T(8,128)(2,1)} %get-tuple-element.339) | copy-start | bytes 786436 | tf_op jit(solution)/shard_map/while
  174.1 34.6 %all-reduce.5.cloned.1.call-start = ((), (), s32[]{:S(2)}) async-start(), calls=%async_computation | async-start | bytes 1572864 | tf_op jit(solution)/shard_map/while/body/eval_jaxpr/psum | solution.py:74
  174.1 7.8 %copy-start.5 = (bf16[256,512]{1,0:T(8,128)(2,1)S(1)}, bf16[256,512]{1,0:T(8,128)(2,1)}, u32[]{:S(2)}) copy-start(bf16[256,512]{1,0:T(8,128)(2,1)} %get-tuple-element.413) | copy-start | bytes 786436 | tf_op jit(solution)/shard_map/while
  174.1 7.8 %copy-start.6 = (bf16[256,512]{1,0:T(8,128)(2,1)S(1)}, bf16[256,512]{1,0:T(8,128)(2,1)}, u32[]{:S(2)}) copy-start(bf16[256,512]{1,0:T(8,128)(2,1)} %get-tuple-element.381) | copy-start | bytes 786436 | tf_op jit(solution)/shard_map/while
  212.4 4.8 %copy-start.1 = (bf16[512,256]{1,0:T(8,128)(2,1)S(1)}, bf16[512,256]{1,0:T(8,128)(2,1)}, u32[]{:S(2)}) copy-start(bf16[512,256]{1,0:T(8,128)(2,1)} %get-tuple-element.339) | copy-start | bytes 786436 | tf_op jit(solution)/shard_map/while
  226.1 34.7 %all-reduce.5.cloned.1.call-start = ((), (), s32[]{:S(2)}) async-start(), calls=%async_computation | async-start | bytes 1572864 | tf_op jit(solution)/shard_map/while/body/eval_jaxpr/psum | solution.py:74
  226.2 7.8 %copy-start.5 = (bf16[256,512]{1,0:T(8,128)(2,1)S(1)}, bf16[256,512]{1,0:T(8,128)(2,1)}, u32[]{:S(2)}) copy-start(bf16[256,512]{1,0:T(8,128)(2,1)} %get-tuple-element.413) | copy-start | bytes 786436 | tf_op jit(solution)/shard_map/while
  226.2 7.8 %copy-start.6 = (bf16[256,512]{1,0:T(8,128)(2,1)S(1)}, bf16[256,512]{1,0:T(8,128)(2,1)}, u32[]{:S(2)}) copy-start(bf16[256,512]{1,0:T(8,128)(2,1)} %get-tuple-element.381) | copy-start | bytes 786436 | tf_op jit(solution)/shard_map/while
  278.3 34.6 %all-reduce.5.cloned.1.call-start = ((), (), s32[]{:S(2)}) async-start(), calls=%async_computation | async-start | bytes 1572864 | tf_op jit(solution)/shard_map/while/body/eval_jaxpr/psum | solution.py:74
  278.3 7.8 %copy-start.5 = (bf16[256,512]{1,0:T(8,128)(2,1)S(1)}, bf16[256,512]{1,0:T(8,128)(2,1)}, u32[]{:S(2)}) copy-start(bf16[256,512]{1,0:T(8,128)(2,1)} %get-tuple-element.413) | copy-start | bytes 786436 | tf_op jit(solution)/shard_map/while
  278.3 7.8 %copy-start.6 = (bf16[256,512]{1,0:T(8,128)(2,1)S(1)}, bf16[256,512]{1,0:T(8,128)(2,1)}, u32[]{:S(2)}) copy-start(bf16[256,512]{1,0:T(8,128)(2,1)} %get-tuple-element.381) | copy-start | bytes 786436 | tf_op jit(solution)/shard_map/while
  316.7 4.8 %copy-start.1 = (bf16[512,256]{1,0:T(8,128)(2,1)S(1)}, bf16[512,256]{1,0:T(8,128)(2,1)}, u32[]{:S(2)}) copy-start(bf16[512,256]{1,0:T(8,128)(2,1)} %get-tuple-element.339) | copy-start | bytes 786436 | tf_op jit(solution)/shard_map/while
  330.4 34.6 %all-reduce.5.cloned.1.call-start = ((), (), s32[]{:S(2)}) async-start(), calls=%async_computation | async-start | bytes 1572864 | tf_op jit(solution)/shard_map/while/body/eval_jaxpr/psum | solution.py:74
  330.4 7.8 %copy-start.5 = (bf16[256,512]{1,0:T(8,128)(2,1)S(1)}, bf16[256,512]{1,0:T(8,128)(2,1)}, u32[]{:S(2)}) copy-start(bf16[256,512]{1,0:T(8,128)(2,1)} %get-tuple-element.413) | copy-start | bytes 786436 | tf_op jit(solution)/shard_map/while
  330.4 7.8 %copy-start.6 = (bf16[256,512]{1,0:T(8,128)(2,1)S(1)}, bf16[256,512]{1,0:T(8,128)(2,1)}, u32[]{:S(2)}) copy-start(bf16[256,512]{1,0:T(8,128)(2,1)} %get-tuple-element.381) | copy-start | bytes 786436 | tf_op jit(solution)/shard_map/while
  368.8 4.8 %copy-start.1 = (bf16[512,256]{1,0:T(8,128)(2,1)S(1)}, bf16[512,256]{1,0:T(8,128)(2,1)}, u32[]{:S(2)}) copy-start(bf16[512,256]{1,0:T(8,128)(2,1)} %get-tuple-element.339) | copy-start | bytes 786436 | tf_op jit(solution)/shard_map/while
  382.5 34.6 %all-reduce.5.cloned.1.call-start = ((), (), s32[]{:S(2)}) async-start(), calls=%async_computation | async-start | bytes 1572864 | tf_op jit(solution)/shard_map/while/body/eval_jaxpr/psum | solution.py:74
  382.5 7.8 %copy-start.5 = (bf16[256,512]{1,0:T(8,128)(2,1)S(1)}, bf16[256,512]{1,0:T(8,128)(2,1)}, u32[]{:S(2)}) copy-start(bf16[256,512]{1,0:T(8,128)(2,1)} %get-tuple-element.413) | copy-start | bytes 786436 | tf_op jit(solution)/shard_map/while
  382.5 7.8 %copy-start.6 = (bf16[256,512]{1,0:T(8,128)(2,1)S(1)}, bf16[256,512]{1,0:T(8,128)(2,1)}, u32[]{:S(2)}) copy-start(bf16[256,512]{1,0:T(8,128)(2,1)} %get-tuple-element.381) | copy-start | bytes 786436 | tf_op jit(solution)/shard_map/while
  (18 other events, 74.7 us)
Sparse Core Ops, SparseCore 0:
  31.2 21.1 all-reduce.4
  84.0 20.4 all-reduce.4
  136.1 20.4 all-reduce.4
  188.2 20.4 all-reduce.4
  240.4 20.4 all-reduce.4
  292.5 20.4 all-reduce.4
  344.5 20.4 all-reduce.4
  396.6 20.4 all-reduce.4
where the time goes:
time: 447 us; the launch traced here: 441 us
  waiting for transfers between devices  152 us (34%)
  matrix products  134 us (30%)
  other arithmetic  125 us (28%)
  local copies, waits for them, and re-layouts  15.6 us (3%)
  between operations  14.2 us (3%)
    psum x8, waiting for transfers between devices, combine(): lax.psum(partials[0].astype(jnp.bfloat16), 'rows').astype(jnp.float32)  152 us
    dot_general x32, matrix products, product(): return jnp.dot(first_op, second_op, preferred_element_type=jnp.float32)  68.3 us
    convert_element_type x24, other arithmetic, refresh(): as_bf16 = tuple((weight.astype(jnp.bfloat16) for weight in master))  51.8 us
    dot_general x24, matrix products, contract_rows(): lax.dot_general(first_op, second_op, (((0,), (0,)), ((), ())), preferred_...  51 us
    reduce_sum x19, other arithmetic, column_norms(): return jnp.sqrt(jnp.sum(weight * weight, axis=0) + 1e-06)  32.7 us
    dynamic_update_slice x8, other arithmetic, body(): _, outputs = lax.scan(advance, start_pair, inputs)  20.6 us
    reduce_sum x16, other arithmetic, normalize_rows(): jnp.mean(matrix * matrix, axis=-1, keepdims=True) + epsilon  18.1 us
    dot_general x8, matrix products, against_rows(): lax.dot_general(first_op, second_op, (((1,), (1,)), ((), ())), preferred_...  15.1 us
  transfers between devices with their start and end apart: 8, of which 8 were waited for; matrix products, arithmetic and copies ran while one was open for 3% of the time, Pallas kernels for 0%

commit v1 on v0

--- a/solution.py
+++ b/solution.py
@@ -1,7 +1,269 @@
+import functools
+
 import jax
 import jax.numpy as jnp
 from jax import lax
+from jax.experimental import pallas as pl
+from jax.experimental.pallas import tpu as pltpu
 from jax.sharding import PartitionSpec as P
+
+MESH = pl.DeviceIdType.MESH
+VMEM_LIMIT = 60 * 1024 * 1024
+
+
+def matmul(first_op, second_op):
+    return jnp.dot(first_op, second_op, preferred_element_type=jnp.float32)
+
+
+def matmul_nt(first_op, second_op):
+    return lax.dot_general(
+        first_op, second_op, (((1,), (1,)), ((), ())), preferred_element_type=jnp.float32
+    )
+
+
+def unit_rows(matrix, epsilon):
+    matrix = matrix.astype(jnp.float32)
+    mean = jnp.mean(matrix * matrix, axis=-1, keepdims=True)
+    return (matrix * lax.rsqrt(mean + epsilon)).astype(jnp.bfloat16)
+
+
+def sigmoid(x):
+    return 0.5 * jnp.tanh(0.5 * x) + 0.5
+
+
+def chain_kernel(
+    steps, slots, blocks, row_devices,
+    counts_ref, rate_ref, q_hbm, k_hbm, v_hbm, w1_ref, w3_ref, w2_ref, out_ref,
+    q_in, k_in, v_in, k_all, v_all, n_own, n_peer, state, sums_own, sums_peer,
+    norm13, norm2, load_sem, send_sem, recv_sem,
+):
+    rows = q_in.shape[1]
+    half = w2_ref.shape[1] // 2
+    me = lax.axis_index("rows")
+    peer = {"rows": 1 - me}
+    seq = lax.axis_index("seq")
+    step_rate = rate_ref[0] / (rows * row_devices)
+    total_blocks = slots * blocks
+
+    def local(src, dst, at):
+        return pltpu.make_async_copy(src, dst, load_sem.at[at])
+
+    first = pl.ds(0, 1)
+    rest = pl.ds(1, total_blocks - 1)
+    loads = [
+        local(k_hbm.at[first], k_in.at[first], 0),
+        local(v_hbm.at[first], v_in.at[first], 1),
+        local(k_hbm.at[rest], k_in.at[rest], 2),
+        local(v_hbm.at[rest], v_in.at[rest], 3),
+        local(q_hbm, q_in, 4),
+    ]
+    for load in loads:
+        load.start()
+
+    barrier = pltpu.get_barrier_semaphore()
+    pl.semaphore_signal(barrier, inc=1, device_id=peer, device_id_type=MESH)
+
+    def where_at(t):
+        block = jnp.int32(0)
+        begins = t == 0
+        offset = jnp.int32(0)
+        for slot in range(slots):
+            begins = begins | (t == offset)
+            inside = jnp.minimum(jnp.maximum(t - offset, 0), blocks - 1)
+            block = jnp.where(t >= offset, slot * blocks + inside, block)
+            offset = offset + counts_ref[seq * slots + slot]
+        return block, begins
+
+    def remote(src, dst, kind, t):
+        return pltpu.make_async_remote_copy(
+            src_ref=src, dst_ref=dst, send_sem=send_sem.at[kind, t], recv_sem=recv_sem.at[kind, t],
+            device_id=peer, device_id_type=MESH,
+        )
+
+    mine, theirs = pl.ds(0, rows), pl.ds(rows, rows)
+    gates, downs = pl.ds(0, 2 * half), pl.ds(2 * half, half)
+
+    def key_copy(t):
+        return remote(k_all.at[t, mine], k_all.at[t, theirs], 0, t)
+
+    def value_copy(t):
+        return remote(v_all.at[t, mine], v_all.at[t, theirs], 1, t)
+
+    def sums_copy(t):
+        return remote(sums_own.at[t], sums_peer.at[t], 2, t)
+
+    def gates_copy(t):
+        return remote(n_own.at[t + 1, gates], n_peer.at[t, gates], 3, t)
+
+    def downs_copy(t):
+        return remote(n_own.at[t + 1, downs], n_peer.at[t, downs], 4, t)
+
+    def prepare(t, block):
+        v_all[t, mine] = v_in[block]
+        value_copy(t).start()
+        k_all[t, mine] = unit_rows(k_in[block], 1e-06)
+        key_copy(t).start()
+
+    units = pl.ds(pl.multiple_of(me * half, half), half)
+    start_1 = w1_ref[0, :, units].astype(jnp.float32).T
+    start_3 = w3_ref[0, :, units].astype(jnp.float32).T
+    start_2 = w2_ref[0, units, :].astype(jnp.float32)
+    start = jnp.concatenate([start_1, start_3, start_2], axis=0)
+    state[0] = start
+    n_own[0] = start.astype(jnp.bfloat16)
+    start_13 = start[: 2 * half]
+    norm13[...] = jnp.sqrt(jnp.sum(start_13 * start_13, axis=1, keepdims=True) + 1e-06)
+    full_2 = w2_ref[0].astype(jnp.float32)
+    norm2[...] = jnp.sqrt(jnp.sum(full_2 * full_2, axis=0, keepdims=True) + 1e-06)
+
+    loads[0].wait()
+    loads[1].wait()
+    pl.semaphore_wait(barrier, 1)
+    prepare(0, 0)
+    for load in loads[2:]:
+        load.wait()
+
+    def answer(t):
+        block, _ = where_at(t)
+        query = unit_rows(q_in[block], 1e-06)
+        own, other = n_own[t + 1], n_peer[t]
+        hidden = []
+        for weights in (own, other):
+            both = matmul_nt(query, weights[: 2 * half])
+            gate, up = both[:, :half], both[:, half:]
+            hidden.append((gate * sigmoid(gate) * up).astype(jnp.bfloat16))
+        result = matmul(
+            jnp.concatenate(hidden, axis=1),
+            jnp.concatenate([own[2 * half :], other[2 * half :]], axis=0),
+        )
+        out_ref[t] = unit_rows(result, 1e-05)
+
+    def step(t, carry):
+        @pl.when(t + 1 < steps)
+        def _():
+            prepare(t + 1, where_at(t + 1)[0])
+
+        _, begins = where_at(t)
+        from_state = jnp.where(begins, 0, 1)
+        from_n = jnp.where(begins, 0, t)
+        key_copy(t).wait_recv()
+        value_copy(t).wait_recv()
+        keys, values = k_all[t], v_all[t]
+        both = matmul_nt(n_own[from_n, gates], keys)
+        d_hidden = matmul_nt(n_own[from_n, downs], values)
+        gate, up = both[:half], both[half:]
+        sig = sigmoid(gate)
+        act = gate * sig
+        hidden = (act * up).astype(jnp.bfloat16)
+        d_gate = (d_hidden * up * (sig + act - act * sig)).astype(jnp.bfloat16)
+        d_up = (d_hidden * act).astype(jnp.bfloat16)
+
+        moved_2 = state[from_state, downs] + step_rate * matmul(hidden, values)
+        squares = moved_2 * moved_2
+        sums_own[t] = jnp.sum(squares.reshape(half // 8, 8, squares.shape[1]), axis=0)
+        sums_copy(t).start()
+
+        moved_13 = state[from_state, gates] + step_rate * matmul(
+            jnp.concatenate([d_gate, d_up], axis=0), keys
+        )
+        norm = jnp.sum(moved_13 * moved_13, axis=1, keepdims=True) + 1e-06
+        new_13 = moved_13 * (norm13[...] * lax.rsqrt(norm))
+        state[1, gates] = new_13
+        state[1, downs] = moved_2
+        n_own[t + 1, gates] = new_13.astype(jnp.bfloat16)
+        gates_copy(t).start()
+
+        @pl.when(t > 0)
+        def _():
+            gates_copy(t - 1).wait_recv()
+            downs_copy(t - 1).wait_recv()
+            answer(t - 1)
+
+        sums_copy(t).wait_recv()
+        norm = jnp.sum(sums_own[t] + sums_peer[t], axis=0, keepdims=True) + 1e-06
+        new_2 = state[1, downs] * (norm2[...] * lax.rsqrt(norm))
+        state[1, downs] = new_2
+        n_own[t + 1, downs] = new_2.astype(jnp.bfloat16)
+        downs_copy(t).start()
+        return carry
+
+    lax.fori_loop(0, steps, step, 0)
+    last = steps - 1
+    gates_copy(last).wait_recv()
+    downs_copy(last).wait_recv()
+    answer(last)
+
+    def finish(t, carry):
+        for copy in (key_copy, value_copy, sums_copy, gates_copy, downs_copy):
+            copy(t).wait_send()
+        return carry
+
+    lax.fori_loop(0, steps, finish, 0)
+
+
+def chain(steps, collective_id, queries, keys, values, counts, rate, w_first, w_third, w_second):
+    slots, blocks, rows, width = queries.shape
+    row_devices = lax.axis_size("rows")
+    hidden = w_second.shape[1]
+    half = hidden // 2
+    total = slots * blocks
+    flat = (total, rows, width)
+    smem = pl.BlockSpec(memory_space=pltpu.SMEM)
+    vmem = pl.BlockSpec(memory_space=pltpu.VMEM)
+    hbm = pl.BlockSpec(memory_space=pl.ANY)
+    bf16, f32 = jnp.bfloat16, jnp.float32
+    return pl.pallas_call(
+        functools.partial(chain_kernel, steps, slots, blocks, row_devices),
+        out_shape=jax.ShapeDtypeStruct(flat, bf16),
+        in_specs=[smem, smem, hbm, hbm, hbm, vmem, vmem, vmem],
+        out_specs=vmem,
+        scratch_shapes=[
+            pltpu.VMEM(flat, bf16),
+            pltpu.VMEM(flat, bf16),
+            pltpu.VMEM(flat, bf16),
+            pltpu.VMEM((steps, 2 * rows, width), bf16),
+            pltpu.VMEM((steps, 2 * rows, width), bf16),
+            pltpu.VMEM((steps + 1, 3 * half, width), bf16),
+            pltpu.VMEM((steps, 3 * half, width), bf16),
+            pltpu.VMEM((2, 3 * half, width), f32),
+            pltpu.VMEM((steps, 8, width), f32),
+            pltpu.VMEM((steps, 8, width), f32),
+            pltpu.VMEM((2 * half, 1), f32),
+            pltpu.VMEM((1, width), f32),
+            pltpu.SemaphoreType.DMA((5,)),
+            pltpu.SemaphoreType.DMA((5, steps)),
+            pltpu.SemaphoreType.DMA((5, steps)),
+        ],
+        compiler_params=pltpu.CompilerParams(
+            collective_id=collective_id, has_side_effects=True, vmem_limit_bytes=VMEM_LIMIT
+        ),
+        cost_estimate=pl.CostEstimate(
+            flops=steps * 18 * rows * width * hidden,
+            bytes_accessed=4 * 2 * total * rows * width,
+            transcendentals=steps * 2 * rows * hidden,
+        ),
+        name="chain",
+    )(
+        counts, rate, queries.reshape(flat), keys.reshape(flat), values.reshape(flat),
+        w_first, w_third, w_second,
+    )
+
+
+def pair_body(queries, keys, values, counts, rate, w_first, w_third, w_second):
+    slots, blocks, rows, width = queries.shape
+    total = slots * blocks
+    in_order = chain(total, 0, queries, keys, values, counts, rate, w_first, w_third, w_second)
+    group = lax.axis_index("seq")
+    own_counts = lax.dynamic_slice_in_dim(counts, group * slots, slots)
+    block_ids = jnp.arange(blocks, dtype=jnp.int32)
+    parts = []
+    offset = jnp.int32(0)
+    for slot in range(slots):
+        part = lax.dynamic_slice_in_dim(in_order, offset, blocks)
+        live = (block_ids < own_counts[slot])[:, None, None]
+        parts.append(jnp.where(live, part, jnp.zeros_like(part)))
+        offset = offset + own_counts[slot]
+    return jnp.stack(parts)
 
 
 def normalize_rows(matrix, epsilon):
@@ -124,9 +386,15 @@
     return outputs.reshape(queries.shape)
 
 
+def any_body(queries, keys, values, counts, rate, w_first, w_third, w_second):
+    pair = lax.axis_size("rows") == 2 and w_second.shape[1] % 256 == 0 and queries.shape[2] % 16 == 0
+    form = pair_body if pair else body
+    return form(queries, keys, values, counts, rate, w_first, w_third, w_second)
+
+
 def solution(mesh):
     return jax.shard_map(
-        body,
+        any_body,
         mesh=mesh,
         in_specs=(
             P("seq", None, "rows", "head"),

time: 447 us -> 34.5 us (0.08); the launches traced: 441 us -> 34.2 us
  waiting for transfers between devices: 152 us -> 0 us
  matrix products: 134 us -> 0 us
  other arithmetic: 125 us -> 4.96 us
  Pallas kernels: 0 us -> 25.4 us
  local copies, waits for them, and re-layouts: 15.6 us -> 1.32 us
  between operations: 14.2 us -> 2.57 us
    psum x8 -> x0, waiting for transfers between devices: 152 us -> none  [combine(): lax.psum(partials[0].astype(jnp.bfloat16), 'rows').astype(jnp.float32)]
    dot_general x64 -> x0, matrix products: 134 us -> none  [the longest x32 68.3 us: product(): return jnp.dot(first_op, second_op, preferred_element_type=jnp.float32)]
    convert_element_type x26 -> x0, other arithmetic: 52.9 us -> none  [the longest x24 51.8 us: refresh(): as_bf16 = tuple((weight.astype(jnp.bfloat16) for weight in master))]
    reduce_sum x35 -> x0, other arithmetic: 50.7 us -> none  [the longest x19 32.7 us: column_norms(): return jnp.sqrt(jnp.sum(weight * weight, axis=0) + 1e-06)]
    pallas_call x0 -> x1, Pallas kernels: none -> 25.4 us  [chain(): pl.pallas_call(functools.partial(chain_kernel, steps, slots, blocks, row_...]
    dynamic_update_slice x8 -> x0, other arithmetic: 20.6 us -> none  [body(): _, outputs = lax.scan(advance, start_pair, inputs)]
    dynamic_slice x17 -> x1, local copies, waits for them, and re-layouts: 10.8 us -> 0.73 us  [pair_body(): own_counts = lax.dynamic_slice_in_dim(counts, group * slots, slots)]
  transfers between devices with their start and end apart: 8 -> 0, of which waited for: 8 -> 0; matrix products, arithmetic and copies ran while one was open for 3% -> 0% of each run, Pallas kernels for 0% -> 0%
where the time goes in v1:
time: 34.5 us; the launch traced here: 34.2 us
  Pallas kernels  25.4 us (74%)
  other arithmetic  4.96 us (14%)
  between operations  2.57 us (7%)
  local copies, waits for them, and re-layouts  1.32 us (4%)
    pallas_call x1, Pallas kernels, chain(): pl.pallas_call(functools.partial(chain_kernel, steps, slots, blocks, row_...  25.4 us
    another operation x2, other arithmetic, pair_body(): return jnp.stack(parts)  3.68 us
    lt x1, other arithmetic, pair_body(): live = (block_ids < own_counts[slot])[:, None, None]  1.28 us
    dynamic_slice x1, local copies, waits for them, and re-layouts, pair_body(): own_counts = lax.dynamic_slice_in_dim(counts, group * slots, slots)  0.73 us

profile of v1, /device:TPU:13, one launch (start us, length us, event | category | flops | bytes accessed | tf_op | source)
XLA Modules:
  0.0 34.2 jit_solution(342495292220485758)
XLA Ops:
  0.7 0.7 %dynamic_slice.9 = s32[2]{0:T(128)S(1)} dynamic-slice(s32[8]{0:T(128)} %counts_ref.1, s32[]{:T(128)S(6)} %select_n.13), dynamic_slice_sizes={2} | dynamic-slice | bytes 20 | tf_op jit(solution)/shard_map/dynamic_slice | solution.py:257
  1.4 0.6 %fusion = (s32[1]{0:T(128)}, s32[1]{0:T(128)}) fusion(s32[2]{0:T(128)S(1)} %dynamic_slice.9), kind=kLoop, calls=%fused_computation.5 | loop fusion | bytes 16 | tf_op jit(solution)/shard_map/slice | solution.py:263
  3.9 1.3 %iota_compare_fusion = (pred[4]{0:T(512)(128)(4,1)S(1)}, pred[4]{0:T(512)(128)(4,1)S(1)}) fusion(s32[]{:T(128)} %bitcast.5, s32[]{:T(128)} %bitcast), kind=kLoop, calls=%fused_computation.3 | loop fusion | flops 8 | bytes 16 | tf_op jit(solution)/shard_map/lt | solution.py:263
  5.2 25.4 %chain.1 = bf16[8,320,512]{2,1,0:T(8,128)(2,1)} custom-call(s32[8]{0:T(128)} %counts_ref.1, f32[1]{0:T(128)S(6)} %copy.9.rate_ref, bf16[8,320,512]{2,1,0:T(8,128)(2,1)} %bitcast.9, bf16[8,320,512]{2,1,0:T(8,128)(2,1)} %bitcast.10, bf16[8,320,512]{2,1,0:T(8,128)(2,1)} %bitcast.11, bf16[1,512,256]{2,1,0:T(8,128)(2,1)} %w1_ref.1, bf16[1,512,256]{2,1,0:T(8,128)(2,1)} %w3_ref.1, ...), custom_call_target="tpu_custom_call" | custom-call | flops 6039797760 | bytes 10485760 | tf_op jit(solution)/shard_map/chain/pallas_call | solution.py:215
  30.5 2.0 %select_bitcast_fusion.1 = (bf16[1,4,320,512]{3,2,1,0:T(8,128)(2,1)S(1)}, bf16[1,4,320,512]{3,2,1,0:T(8,128)(2,1)S(1)}) fusion(bf16[8,320,512]{2,1,0:T(8,128)(2,1)} %chain.1, pred[4]{0:T(512)(128)(4,1)S(1)} %get-tuple-element.10, s32[]{:T(128)S(6)} %select_n.15, pred[4]{0:T(512)(128)(4,1)S(1)} %get-tuple-element.9), kind=kLoop, calls=%fused_computation.2 | loop fusion | flops 1310720 | bytes 5242892 | tf_op jit(solution)/shard_map/stack | solution.py:266
  32.5 1.7 %pad_maximum_fusion = bf16[2,4,320,512]{3,2,1,0:T(8,128)(2,1)} fusion(bf16[1,4,320,512]{3,2,1,0:T(8,128)(2,1)S(1)} %get-tuple-element.6, bf16[1,4,320,512]{3,2,1,0:T(8,128)(2,1)S(1)} %get-tuple-element.5), kind=kLoop, calls=%fused_computation | loop fusion | flops 1310720 | bytes 5242880 | tf_op jit(solution)/shard_map/stack | solution.py:266
